TPU v7x, 512 devices: a whole 4x4x16 slice. The times are simulated.
512 devices in a mesh: replica: 64 (over y, z), tensor: 8 (over x, core).
Axes of the slice: x: 4, y: 4, z: 16, core: 2. Of those that a mesh axis runs over, the one named last changes fastest.
Arguments:
- qkv_grads: float32 [64, 64, 18432], P('replica', None, 'tensor'), may hold values from -65 to 65
- proj_grads: float32 [64, 64, 6144], P('replica', None, 'tensor'), may hold values from -65 to 65
- mlp_in_grads: float32 [64, 64, 24576], P('replica', None, 'tensor'), may hold values from -65 to 65
- mlp_out_grads: float32 [64, 64, 24576], P('replica', None, 'tensor'), may hold values from -65 to 65
Outputs:
- qkv_combined: float32 [64, 18432], P('replica', 'tensor')
- proj_combined: float32 [64, 6144], P('replica', 'tensor')
- mlp_in_combined: float32 [64, 24576], P('replica', 'tensor')
- mlp_out_combined: float32 [64, 24576], P('replica', 'tensor')
All inputs are finite; a program needn't handle non-finite values.
Results may differ from a plain program's by a relative error of at most 0.00011.
Values sent between devices are 32-bit elements; how exact they have to be, the bound alone decides.
A program may use at most 64 MiB of HBM per device.

v0:
```python
import jax
import jax.numpy as jnp
from jax import lax
from jax.sharding import PartitionSpec as P

EPSILON = 1e-06


def partner_2(shard, axis, bit):
    return lax.ppermute(shard, axis, [(i, i ^ 1 << bit) for i in range(lax.axis_size(axis))])


def pair_statistics(lower_group, upper_group):
    return jnp.stack(
        [
            jnp.sum(lower_group * upper_group),
            jnp.sum(lower_group * lower_group),
            jnp.sum(upper_group * upper_group),
        ]
    )


def combine_pair(lower_group, upper_group, totals):
    cross = totals[0]
    lower_weight = 1.0 - cross / (2.0 * (totals[1] + EPSILON))
    upper_weight = 1.0 - cross / (2.0 * (totals[2] + EPSILON))
    return lower_weight * lower_group + upper_weight * upper_group


def per_device(qkv_grads, proj_grads, mlp_in_grads, mlp_out_grads):
    tensors = [qkv_grads[0], proj_grads[0], mlp_in_grads[0], mlp_out_grads[0]]
    shapes = [member.shape for member in tensors]
    replicas = lax.axis_size("replica")
    sections = replicas.bit_length() - 1
    replica_index = lax.axis_index("replica")
    block_rows = shapes[0][0] // replicas
    for section_bit in range(sections):
        higher = replica_index >> section_bit & 1 == 1
        partner = partner_2(
            (tensors[0], tensors[1], tensors[2], tensors[3]), "replica", section_bit
        )
        lowers = [jnp.where(higher, theirs, mine) for mine, theirs in zip(tensors, partner)]
        uppers = [jnp.where(higher, mine, theirs) for mine, theirs in zip(tensors, partner)]
        statistics = jnp.stack(
            [
                pair_statistics(lower_group, upper_group)
                for lower_group, upper_group in zip(lowers, uppers)
            ]
        )
        totals = lax.psum(statistics, "tensor")
        tensors = [
            combine_pair(lower_group, upper_group, totals[number])
            for number, (lower_group, upper_group) in enumerate(zip(lowers, uppers))
        ]
    row_start = replica_index * block_rows
    outputs = [lax.dynamic_slice_in_dim(member, row_start, block_rows, 0) for member in tensors]
    return (outputs[0], outputs[1], outputs[2], outputs[3])


def solution(mesh):
    return jax.shard_map(
        per_device,
        mesh=mesh,
        in_specs=(
            P("replica", None, "tensor"),
            P("replica", None, "tensor"),
            P("replica", None, "tensor"),
            P("replica", None, "tensor"),
        ),
        out_specs=(
            P("replica", "tensor"),
            P("replica", "tensor"),
            P("replica", "tensor"),
            P("replica", "tensor"),
        ),
        check_vma=False,
    )
```

profile of v0, /device:TPU:1, one launch (start us, length us, event | category | flops | bytes accessed | tf_op | source)
XLA Modules:
  0.0 886.7 jit_solution(8806559948268977775)
XLA Ops:
  0.6 4.5 collective-permute-start
  7.1 3.4 collective-permute-start.3
  12.4 5.7 collective-permute-done.1
  21.6 3.8 maximum_bitcast_fusion
  25.4 9.6 %collective-permute-done.3 = f32[64,3072]{1,0:T(8,128)S(1)} collective-permute-done((f32[64,3072]{1,0:T(8,128)}, f32[64,3072]{1,0:T(8,128)S(1)}, u32[]{:S(2)}, u32[]{:S(2)}) %collective-permute-start.3) | collective-permute-done | bytes 786464 | tf_op jit(solution)/shard_map/ppermute | solution.py:10
  35.9 15.9 %collective-permute-done.2 = f32[64,3072]{1,0:T(8,128)} collective-permute-done((f32[64,3072]{1,0:T(8,128)}, f32[64,3072]{1,0:T(8,128)}, u32[]{:S(2)}, u32[]{:S(2)}) %collective-permute-start.2) | collective-permute-done | bytes 786464 | tf_op jit(solution)/shard_map/ppermute | solution.py:10
  51.8 2.6 multiply_reduce_fusion.32
  54.4 2.0 maximum_bitcast_fusion.3
  58.4 17.6 %psum.42 = f32[4,3]{1,0:T(4,128)S(1)} all-reduce(f32[4,3]{1,0:T(4,128)S(1)} %pad_maximum_fusion), channel_id=1, replica_groups=mesh['replica'=64,'tensor'=8] {'tensor'}, use_global_device_ids=true, to_apply=%region_12.13 | all-reduce | flops 12 | bytes 96 | tf_op jit(solution)/shard_map/psum | solution.py:50
  80.6 4.9 collective-permute-start.4
  95.2 4.3 collective-permute-start.5
  101.5 68.2 %collective-permute-done.5 = f32[64,768]{1,0:T(8,128)S(1)} collective-permute-done((f32[64,768]{1,0:T(8,128)S(1)}, f32[64,768]{1,0:T(8,128)S(1)}, u32[]{:S(2)}, u32[]{:S(2)}) %collective-permute-start.5) | collective-permute-done | bytes 196640 | tf_op jit(solution)/shard_map/ppermute | solution.py:10
  170.4 2.0 maximum_bitcast_fusion.5
  174.2 2.0 maximum_bitcast_fusion.4
  177.1 2.0 maximum_bitcast_fusion.7
  179.2 7.4 collective-permute-done.6
  187.5 2.0 maximum_bitcast_fusion.6
  189.5 13.5 %psum.43 = f32[4,3]{1,0:T(4,128)S(1)} all-reduce(f32[4,3]{1,0:T(4,128)S(1)} %pad_maximum_fusion.1), channel_id=1, replica_groups=mesh['replica'=64,'tensor'=8] {'tensor'}, use_global_device_ids=true, to_apply=%region_25.26 | all-reduce | flops 12 | bytes 96 | tf_op jit(solution)/shard_map/psum | solution.py:50
  207.6 8.8 collective-permute-start.8
  226.0 7.3 collective-permute-start.9
  235.3 217.5 %collective-permute-done.9 = f32[64,768]{1,0:T(8,128)S(1)} collective-permute-done((f32[64,768]{1,0:T(8,128)S(1)}, f32[64,768]{1,0:T(8,128)S(1)}, u32[]{:S(2)}, u32[]{:S(2)}) %collective-permute-start.9) | collective-permute-done | bytes 196640 | tf_op jit(solution)/shard_map/ppermute | solution.py:10
  457.2 2.0 maximum_bitcast_fusion.8
  462.2 7.4 collective-permute-done.10
  472.6 12.3 %psum.44 = f32[4,3]{1,0:T(4,128)S(1)} all-reduce(f32[4,3]{1,0:T(4,128)S(1)} %pad_maximum_fusion.2), channel_id=1, replica_groups=mesh['replica'=64,'tensor'=8] {'tensor'}, use_global_device_ids=true, to_apply=%region_38.39 | all-reduce | flops 12 | bytes 96 | tf_op jit(solution)/shard_map/psum | solution.py:50
  489.5 113.9 %collective-permute-start.12 = (f32[64,2304]{1,0:T(8,128)S(1)}, f32[64,2304]{1,0:T(8,128)S(1)}, u32[]{:S(2)}, u32[]{:S(2)}) collective-permute-start(f32[64,2304]{1,0:T(8,128)S(1)} %multiply_add_fusion.12), channel_id=1, source_target_pairs={{0,64},{8,72},{16,80},{24,88},{32,96},{40,104},{48,112},{56,120},{... | collective-permute-start | bytes 1769480 | tf_op jit(solution)/shard_map/ppermute | solution.py:10
  613.0 12.1 %collective-permute-start.13 = (f32[64,768]{1,0:T(8,128)S(1)}, f32[64,768]{1,0:T(8,128)S(1)}, u32[]{:S(2)}, u32[]{:S(2)}) collective-permute-start(f32[64,768]{1,0:T(8,128)S(1)} %multiply_add_fusion.17), channel_id=1, source_target_pairs={{0,64},{8,72},{16,80},{24,88},{32,96},{40,104},{48,112},{56,120},{... | collective-permute-start | bytes 589832 | tf_op jit(solution)/shard_map/ppermute | solution.py:10
  627.1 53.1 %collective-permute-done.13 = f32[64,768]{1,0:T(8,128)S(1)} collective-permute-done((f32[64,768]{1,0:T(8,128)S(1)}, f32[64,768]{1,0:T(8,128)S(1)}, u32[]{:S(2)}, u32[]{:S(2)}) %collective-permute-start.13) | collective-permute-done | bytes 196640 | tf_op jit(solution)/shard_map/ppermute | solution.py:10
  680.9 2.0 maximum_bitcast_fusion.13
  684.6 2.0 maximum_bitcast_fusion.12
  687.6 2.0 maximum_bitcast_fusion.15
  689.7 15.3 %collective-permute-done.14 = f32[64,3072]{1,0:T(8,128)S(1)} collective-permute-done((f32[64,3072]{1,0:T(8,128)S(1)}, f32[64,3072]{1,0:T(8,128)S(1)}, u32[]{:S(2)}, u32[]{:S(2)}) %collective-permute-start.14) | collective-permute-done | bytes 786464 | tf_op jit(solution)/shard_map/ppermute | solution.py:10
  705.9 2.0 maximum_bitcast_fusion.14
  707.9 13.4 %psum.45 = f32[4,3]{1,0:T(4,128)S(1)} all-reduce(f32[4,3]{1,0:T(4,128)S(1)} %pad_maximum_fusion.3), channel_id=1, replica_groups=mesh['replica'=64,'tensor'=8] {'tensor'}, use_global_device_ids=true, to_apply=%region_51.52 | all-reduce | flops 12 | bytes 96 | tf_op jit(solution)/shard_map/psum | solution.py:50
  725.8 3.2 collective-permute-start.16
  731.7 2.1 collective-permute-start.19
  738.7 3.2 collective-permute-start.17
  742.0 2.1 collective-permute-start.18
  744.1 18.9 %collective-permute-done.17 = f32[64,768]{1,0:T(8,128)S(1)} collective-permute-done((f32[64,768]{1,0:T(8,128)S(1)}, f32[64,768]{1,0:T(8,128)S(1)}, u32[]{:S(2)}, u32[]{:S(2)}) %collective-permute-start.17) | collective-permute-done | bytes 196640 | tf_op jit(solution)/shard_map/ppermute | solution.py:10
  763.7 2.0 maximum_bitcast_fusion.17
  770.5 2.0 maximum_bitcast_fusion.19
  772.5 7.4 collective-permute-done.18
  780.8 2.0 maximum_bitcast_fusion.18
  782.9 13.3 %psum.46 = f32[4,3]{1,0:T(4,128)S(1)} all-reduce(f32[4,3]{1,0:T(4,128)S(1)} %pad_maximum_fusion.4), channel_id=1, replica_groups=mesh['replica'=64,'tensor'=8] {'tensor'}, use_global_device_ids=true, to_apply=%region_64.65 | all-reduce | flops 12 | bytes 96 | tf_op jit(solution)/shard_map/psum | solution.py:50
  800.7 4.8 collective-permute-start.20
  815.1 4.8 collective-permute-start.21
  822.0 17.4 %collective-permute-done.21 = f32[64,768]{1,0:T(8,128)S(1)} collective-permute-done((f32[64,768]{1,0:T(8,128)S(1)}, f32[64,768]{1,0:T(8,128)S(1)}, u32[]{:S(2)}, u32[]{:S(2)}) %collective-permute-start.21) | collective-permute-done | bytes 196640 | tf_op jit(solution)/shard_map/ppermute | solution.py:10
  848.9 7.4 collective-permute-done.22
  859.2 13.3 %psum.47 = f32[4,3]{1,0:T(4,128)S(1)} all-reduce(f32[4,3]{1,0:T(4,128)S(1)} %pad_maximum_fusion.5), channel_id=1, replica_groups=mesh['replica'=64,'tensor'=8] {'tensor'}, use_global_device_ids=true, to_apply=%region_77.78 | all-reduce | flops 12 | bytes 96 | tf_op jit(solution)/shard_map/psum | solution.py:50
  (96 shorter events, 78.9 us)
Async XLA Ops:
  0.6 19.2 %copy-start.3 = (f32[1,64,2304]{2,1,0:T(8,128)S(1)}, f32[1,64,2304]{2,1,0:T(8,128)}, u32[]{:S(2)}) copy-start(f32[1,64,2304]{2,1,0:T(8,128)} %param.4) | copy-start | bytes 1769476
  0.6 19.2 %collective-permute-start = (f32[64,2304]{1,0:T(8,128)}, f32[64,2304]{1,0:T(8,128)S(1)}, u32[]{:S(2)}, u32[]{:S(2)}) collective-permute-start(f32[64,2304]{1,0:T(8,128)} %bitcast.190), channel_id=1, source_target_pairs={{0,8},{8,0},{16,24},{24,16},{32,40},{40,32},{48,56},{56,48},{64,72... | collective-permute-start | bytes 1769480 | tf_op jit(solution)/shard_map/ppermute | solution.py:10
  5.2 13.0 %collective-permute-start.1 = (f32[64,768]{1,0:T(8,128)}, f32[64,768]{1,0:T(8,128)S(1)}, u32[]{:S(2)}, u32[]{:S(2)}) collective-permute-start(f32[64,768]{1,0:T(8,128)} %bitcast.191), channel_id=1, source_target_pairs={{0,8},{8,0},{16,24},{24,16},{32,40},{40,32},{48,56},{56,48},{64,72... | collective-permute-start | bytes 589832 | tf_op jit(solution)/shard_map/ppermute | solution.py:10
  7.1 27.9 %collective-permute-start.3 = (f32[64,3072]{1,0:T(8,128)}, f32[64,3072]{1,0:T(8,128)S(1)}, u32[]{:S(2)}, u32[]{:S(2)}) collective-permute-start(f32[64,3072]{1,0:T(8,128)} %bitcast.188), channel_id=1, source_target_pairs={{0,8},{8,0},{16,24},{24,16},{32,40},{40,32},{48,56},{56,48},{64,72... | collective-permute-start | bytes 2359304 | tf_op jit(solution)/shard_map/ppermute | solution.py:10
  10.5 41.4 %collective-permute-start.2 = (f32[64,3072]{1,0:T(8,128)}, f32[64,3072]{1,0:T(8,128)}, u32[]{:S(2)}, u32[]{:S(2)}) collective-permute-start(f32[64,3072]{1,0:T(8,128)} %bitcast.189), channel_id=1, source_target_pairs={{0,8},{8,0},{16,24},{24,16},{32,40},{40,32},{48,56},{56,48},{64,72... | collective-permute-start | bytes 2359304 | tf_op jit(solution)/shard_map/ppermute | solution.py:10
  19.8 32.1 %copy-start = (f32[1,64,3072]{2,1,0:T(8,128)S(1)}, f32[1,64,3072]{2,1,0:T(8,128)}, u32[]{:S(2)}) copy-start(f32[1,64,3072]{2,1,0:T(8,128)} %param.7) | copy-start | bytes 2359300
  19.8 32.1 %copy-start.1 = (f32[1,64,3072]{2,1,0:T(8,128)S(1)}, f32[1,64,3072]{2,1,0:T(8,128)}, u32[]{:S(2)}) copy-start(f32[1,64,3072]{2,1,0:T(8,128)} %param.6) | copy-start | bytes 2359300
  35.0 0.9 copy-start.2
  80.6 91.8 %collective-permute-start.4 = (f32[64,2304]{1,0:T(8,128)S(1)}, f32[64,2304]{1,0:T(8,128)S(1)}, u32[]{:S(2)}, u32[]{:S(2)}) collective-permute-start(f32[64,2304]{1,0:T(8,128)S(1)} %multiply_add_fusion.14), channel_id=1, source_target_pairs={{0,16},{8,24},{16,0},{24,8},{32,48},{40,56},{48,32},{56,40},{64,80... | collective-permute-start | bytes 1769480 | tf_op jit(solution)/shard_map/ppermute | solution.py:10
  88.2 87.9 %collective-permute-start.7 = (f32[64,3072]{1,0:T(8,128)S(1)}, f32[64,3072]{1,0:T(8,128)S(1)}, u32[]{:S(2)}, u32[]{:S(2)}) collective-permute-start(f32[64,3072]{1,0:T(8,128)S(1)} %multiply_add_fusion.8), channel_id=1, source_target_pairs={{0,16},{8,24},{16,0},{24,8},{32,48},{40,56},{48,32},{56,40},{64,80... | collective-permute-start | bytes 2359304 | tf_op jit(solution)/shard_map/ppermute | solution.py:10
  95.2 74.5 %collective-permute-start.5 = (f32[64,768]{1,0:T(8,128)S(1)}, f32[64,768]{1,0:T(8,128)S(1)}, u32[]{:S(2)}, u32[]{:S(2)}) collective-permute-start(f32[64,768]{1,0:T(8,128)S(1)} %multiply_add_fusion.19), channel_id=1, source_target_pairs={{0,16},{8,24},{16,0},{24,8},{32,48},{40,56},{48,32},{56,40},{64,80... | collective-permute-start | bytes 589832 | tf_op jit(solution)/shard_map/ppermute | solution.py:10
  99.6 86.9 %collective-permute-start.6 = (f32[64,3072]{1,0:T(8,128)S(1)}, f32[64,3072]{1,0:T(8,128)S(1)}, u32[]{:S(2)}, u32[]{:S(2)}) collective-permute-start(f32[64,3072]{1,0:T(8,128)S(1)} %multiply_add_fusion.9), channel_id=1, source_target_pairs={{0,16},{8,24},{16,0},{24,8},{32,48},{40,56},{48,32},{56,40},{64,80... | collective-permute-start | bytes 2359304 | tf_op jit(solution)/shard_map/ppermute | solution.py:10
  207.6 247.9 %collective-permute-start.8 = (f32[64,2304]{1,0:T(8,128)S(1)}, f32[64,2304]{1,0:T(8,128)S(1)}, u32[]{:S(2)}, u32[]{:S(2)}) collective-permute-start(f32[64,2304]{1,0:T(8,128)S(1)} %multiply_add_fusion.13), channel_id=1, source_target_pairs={{0,32},{8,40},{16,48},{24,56},{32,0},{40,8},{48,16},{56,24},{64,96... | collective-permute-start | bytes 1769480 | tf_op jit(solution)/shard_map/ppermute | solution.py:10
  219.1 240.1 %collective-permute-start.11 = (f32[64,3072]{1,0:T(8,128)S(1)}, f32[64,3072]{1,0:T(8,128)S(1)}, u32[]{:S(2)}, u32[]{:S(2)}) collective-permute-start(f32[64,3072]{1,0:T(8,128)S(1)} %multiply_add_fusion.6), channel_id=1, source_target_pairs={{0,32},{8,40},{16,48},{24,56},{32,0},{40,8},{48,16},{56,24},{64,96... | collective-permute-start | bytes 2359304 | tf_op jit(solution)/shard_map/ppermute | solution.py:10
  226.0 226.8 %collective-permute-start.9 = (f32[64,768]{1,0:T(8,128)S(1)}, f32[64,768]{1,0:T(8,128)S(1)}, u32[]{:S(2)}, u32[]{:S(2)}) collective-permute-start(f32[64,768]{1,0:T(8,128)S(1)} %multiply_add_fusion.18), channel_id=1, source_target_pairs={{0,32},{8,40},{16,48},{24,56},{32,0},{40,8},{48,16},{56,24},{64,96... | collective-permute-start | bytes 589832 | tf_op jit(solution)/shard_map/ppermute | solution.py:10
  233.3 236.3 %collective-permute-start.10 = (f32[64,3072]{1,0:T(8,128)S(1)}, f32[64,3072]{1,0:T(8,128)S(1)}, u32[]{:S(2)}, u32[]{:S(2)}) collective-permute-start(f32[64,3072]{1,0:T(8,128)S(1)} %multiply_add_fusion.7), channel_id=1, source_target_pairs={{0,32},{8,40},{16,48},{24,56},{32,0},{40,8},{48,16},{56,24},{64,96... | collective-permute-start | bytes 2359304 | tf_op jit(solution)/shard_map/ppermute | solution.py:10
  489.5 193.4 %collective-permute-start.12 = (f32[64,2304]{1,0:T(8,128)S(1)}, f32[64,2304]{1,0:T(8,128)S(1)}, u32[]{:S(2)}, u32[]{:S(2)}) collective-permute-start(f32[64,2304]{1,0:T(8,128)S(1)} %multiply_add_fusion.12), channel_id=1, source_target_pairs={{0,64},{8,72},{16,80},{24,88},{32,96},{40,104},{48,112},{56,120},{... | collective-permute-start | bytes 1769480 | tf_op jit(solution)/shard_map/ppermute | solution.py:10
  606.1 80.6 %collective-permute-start.15 = (f32[64,3072]{1,0:T(8,128)S(1)}, f32[64,3072]{1,0:T(8,128)S(1)}, u32[]{:S(2)}, u32[]{:S(2)}) collective-permute-start(f32[64,3072]{1,0:T(8,128)S(1)} %multiply_add_fusion.4), channel_id=1, source_target_pairs={{0,64},{8,72},{16,80},{24,88},{32,96},{40,104},{48,112},{56,120},{... | collective-permute-start | bytes 2359304 | tf_op jit(solution)/shard_map/ppermute | solution.py:10
  613.0 67.2 %collective-permute-start.13 = (f32[64,768]{1,0:T(8,128)S(1)}, f32[64,768]{1,0:T(8,128)S(1)}, u32[]{:S(2)}, u32[]{:S(2)}) collective-permute-start(f32[64,768]{1,0:T(8,128)S(1)} %multiply_add_fusion.17), channel_id=1, source_target_pairs={{0,64},{8,72},{16,80},{24,88},{32,96},{40,104},{48,112},{56,120},{... | collective-permute-start | bytes 589832 | tf_op jit(solution)/shard_map/ppermute | solution.py:10
  625.1 79.8 %collective-permute-start.14 = (f32[64,3072]{1,0:T(8,128)S(1)}, f32[64,3072]{1,0:T(8,128)S(1)}, u32[]{:S(2)}, u32[]{:S(2)}) collective-permute-start(f32[64,3072]{1,0:T(8,128)S(1)} %multiply_add_fusion.5), channel_id=1, source_target_pairs={{0,64},{8,72},{16,80},{24,88},{32,96},{40,104},{48,112},{56,120},{... | collective-permute-start | bytes 2359304 | tf_op jit(solution)/shard_map/ppermute | solution.py:10
  725.8 39.9 %collective-permute-start.16 = (f32[64,2304]{1,0:T(8,128)S(1)}, f32[64,2304]{1,0:T(8,128)S(1)}, u32[]{:S(2)}, u32[]{:S(2)}) collective-permute-start(f32[64,2304]{1,0:T(8,128)S(1)} %multiply_add_fusion.11), channel_id=1, source_target_pairs={{0,128},{8,136},{16,144},{24,152},{32,160},{40,168},{48,176},{56,1... | collective-permute-start | bytes 1769480 | tf_op jit(solution)/shard_map/ppermute | solution.py:10
  731.7 37.8 %collective-permute-start.19 = (f32[64,3072]{1,0:T(8,128)S(1)}, f32[64,3072]{1,0:T(8,128)S(1)}, u32[]{:S(2)}, u32[]{:S(2)}) collective-permute-start(f32[64,3072]{1,0:T(8,128)S(1)} %multiply_add_fusion.2), channel_id=1, source_target_pairs={{0,128},{8,136},{16,144},{24,152},{32,160},{40,168},{48,176},{56,1... | collective-permute-start | bytes 2359304 | tf_op jit(solution)/shard_map/ppermute | solution.py:10
  738.7 24.3 %collective-permute-start.17 = (f32[64,768]{1,0:T(8,128)S(1)}, f32[64,768]{1,0:T(8,128)S(1)}, u32[]{:S(2)}, u32[]{:S(2)}) collective-permute-start(f32[64,768]{1,0:T(8,128)S(1)} %multiply_add_fusion.16), channel_id=1, source_target_pairs={{0,128},{8,136},{16,144},{24,152},{32,160},{40,168},{48,176},{56,1... | collective-permute-start | bytes 589832 | tf_op jit(solution)/shard_map/ppermute | solution.py:10
  742.0 37.8 %collective-permute-start.18 = (f32[64,3072]{1,0:T(8,128)S(1)}, f32[64,3072]{1,0:T(8,128)S(1)}, u32[]{:S(2)}, u32[]{:S(2)}) collective-permute-start(f32[64,3072]{1,0:T(8,128)S(1)} %multiply_add_fusion.3), channel_id=1, source_target_pairs={{0,128},{8,136},{16,144},{24,152},{32,160},{40,168},{48,176},{56,1... | collective-permute-start | bytes 2359304 | tf_op jit(solution)/shard_map/ppermute | solution.py:10
  800.7 41.4 %collective-permute-start.20 = (f32[64,2304]{1,0:T(8,128)S(1)}, f32[64,2304]{1,0:T(8,128)S(1)}, u32[]{:S(2)}, u32[]{:S(2)}) collective-permute-start(f32[64,2304]{1,0:T(8,128)S(1)} %multiply_add_fusion.10), channel_id=1, source_target_pairs={{0,256},{8,264},{16,272},{24,280},{32,288},{40,296},{48,304},{56,3... | collective-permute-start | bytes 1769480 | tf_op jit(solution)/shard_map/ppermute | solution.py:10
  808.2 37.6 %collective-permute-start.23 = (f32[64,3072]{1,0:T(8,128)S(1)}, f32[64,3072]{1,0:T(8,128)S(1)}, u32[]{:S(2)}, u32[]{:S(2)}) collective-permute-start(f32[64,3072]{1,0:T(8,128)S(1)} %multiply_add_fusion), channel_id=1, source_target_pairs={{0,256},{8,264},{16,272},{24,280},{32,288},{40,296},{48,304},{56,3... | collective-permute-start | bytes 2359304 | tf_op jit(solution)/shard_map/ppermute | solution.py:10
  815.1 24.3 %collective-permute-start.21 = (f32[64,768]{1,0:T(8,128)S(1)}, f32[64,768]{1,0:T(8,128)S(1)}, u32[]{:S(2)}, u32[]{:S(2)}) collective-permute-start(f32[64,768]{1,0:T(8,128)S(1)} %multiply_add_fusion.15), channel_id=1, source_target_pairs={{0,256},{8,264},{16,272},{24,280},{32,288},{40,296},{48,304},{56,3... | collective-permute-start | bytes 589832 | tf_op jit(solution)/shard_map/ppermute | solution.py:10
  820.0 36.2 %collective-permute-start.22 = (f32[64,3072]{1,0:T(8,128)S(1)}, f32[64,3072]{1,0:T(8,128)S(1)}, u32[]{:S(2)}, u32[]{:S(2)}) collective-permute-start(f32[64,3072]{1,0:T(8,128)S(1)} %multiply_add_fusion.1), channel_id=1, source_target_pairs={{0,256},{8,264},{16,272},{24,280},{32,288},{40,296},{48,304},{56,3... | collective-permute-start | bytes 2359304 | tf_op jit(solution)/shard_map/ppermute | solution.py:10
where the time goes:
time: 889 us; the launch traced here: 887 us
  waiting for transfers between devices  451 us (51%)
  starting transfers between devices  199 us (22%)
  other arithmetic  87.1 us (10%)
  blocking collectives  83.3 us (9%)
  between operations  61.5 us (7%)
    ppermute x24, waiting for transfers between devices, partner_2(): lax.ppermute(shard, axis, [(i, i ^ 1 << bit) for i in range(lax.axis_size...  451 us
    ppermute x24, starting transfers between devices, partner_2(): lax.ppermute(shard, axis, [(i, i ^ 1 << bit) for i in range(lax.axis_size...  199 us
    psum x6, blocking collectives, per_device(): totals = lax.psum(statistics, 'tensor')  83.3 us
    another operation x29, other arithmetic, per_device(): jnp.stack([pair_statistics(lower_group, upper_group) for lower_group, upp...  48.1 us
    reduce_sum x23, other arithmetic, pair_statistics(): jnp.sum(lower_group * upper_group)  28 us
  transfers between devices with their start and end apart: 24, of which 13 were waited for; matrix products, arithmetic and copies ran while one was open for 6% of the time, Pallas kernels for 0%

commit v1 on v0

v1 whole, which is shorter than its diff:
```python
import functools

import jax
import jax.numpy as jnp
from jax import lax
from jax.experimental import pallas as pl
from jax.experimental.pallas import tpu as pltpu
from jax.sharding import PartitionSpec as P

EPSILON = 1e-06
LANES = 128
TRUSTED = 0.03
MESH = pl.DeviceIdType.MESH


def lower_weight(cross, norm):
    return 1.0 - cross / (2.0 * (norm + EPSILON))


def tree_weights(gram):
    count = gram.shape[0]
    across = lax.broadcasted_iota(jnp.int32, (count, count), 1)
    down = lax.broadcasted_iota(jnp.int32, (count, count), 0)
    coefficients = jnp.ones((count, 1), jnp.float32)
    doubtful = jnp.zeros((count, 1), jnp.float32)
    scaled = gram
    for level in range(count.bit_length() - 1):
        same = (across >> level) == (down >> level)
        either = (across >> (level + 1)) == (down >> (level + 1))
        own = jnp.where(same, scaled, 0.0)
        sibling = jnp.where(either, scaled, 0.0) - own
        sizes = jnp.abs(own)

        def column_of(terms):
            partial = jnp.sum(terms, axis=0, keepdims=True)
            return jnp.sum(jnp.where(same, partial, 0.0), axis=1, keepdims=True)

        def row_of(terms):
            partial = jnp.sum(terms, axis=1, keepdims=True)
            return jnp.sum(jnp.where(same, partial, 0.0), axis=0, keepdims=True)

        norm = column_of(own)
        column = lower_weight(column_of(sibling), norm)
        row = lower_weight(row_of(sibling), row_of(own))
        doubtful = jnp.maximum(
            doubtful, jnp.where(norm < TRUSTED * column_of(sizes), 1.0, 0.0)
        )
        coefficients = coefficients * column
        scaled = scaled * column * row
    return coefficients, doubtful


def kernel(
    replicas,
    tensors,
    members,
    tiles,
    *refs,
):
    count = sum(len(chunk) for chunk in members)
    chunks = len(members)
    inputs, outs, rest = refs[:count], refs[count : 2 * count], refs[2 * count :]
    (gathered, flags, raw, laid, half_in, half, quarter_in, quarter,
     stat_pair, stat_cluster, gram_rows, gram_cluster, gathered_v,
     in_sem, half_send, half_recv, pair_send, pair_recv, quarter_send, quarter_recv,
     cluster_send, cluster_recv, row_send, row_recv, gram_row_send, gram_row_recv,
     gram_cluster_send, gram_cluster_recv, out_sem) = rest

    groups = replicas // 4
    replica = lax.axis_index("replica")
    tensor = lax.axis_index("tensor")
    group = replica // 4
    local = replica % 4
    bit = local % 2
    high = local // 2
    pair_size, cluster_size = 2 * tensors, 4 * tensors
    pair_me = bit * tensors + tensor
    cluster_me = local * tensors + tensor

    def pair_device(index):
        return (group * 4 + high * 2 + index // tensors, index % tensors)

    def cluster_device(index):
        return (group * 4 + index // tensors, index % tensors)

    def group_device(index):
        return (index * 4 + local, tensor)

    barrier = pltpu.get_barrier_semaphore()

    def greet(size, me, device):
        def one(step, carry):
            pl.semaphore_signal(
                barrier, inc=1, device_id=device((me + step) % size), device_id_type=MESH
            )
            return carry

        lax.fori_loop(1, size, one, 0)

    greet(cluster_size, cluster_me, cluster_device)
    greet(groups, group, group_device)

    input_copies = []
    number = 0
    for chunk, widths in enumerate(members):
        start = 0
        for width in widths:
            input_copies.append(
                pltpu.make_async_copy(
                    inputs[number].at[0],
                    raw.at[chunk, :, pl.ds(start, width * LANES)],
                    in_sem.at[number],
                )
            )
            start += width * LANES
            number += 1
    for copy in input_copies:
        copy.start()

    rows_of_tile = lax.broadcasted_iota(jnp.int32, (tiles, LANES), 0)
    tile_row = lax.broadcasted_iota(jnp.int32, (8, LANES), 0)

    def spans(chunk):
        start = 0
        for width in members[chunk]:
            yield start, start + width
            start += width

    def bring(chunk):
        first = sum(len(widths) for widths in members[:chunk])
        for number in range(first, first + len(members[chunk])):
            input_copies[number].wait()

        def block(step, carry):
            top = pl.multiple_of(step * 8, 8)
            for column in range(tiles):
                laid[chunk, pl.ds(top * tiles + column, 8, stride=tiles), :] = raw[
                    chunk, pl.ds(top, 8), pl.ds(column * LANES, LANES)
                ]
            return carry

        lax.fori_loop(0, replicas // 8, block, 0)

    def half_copies(chunk):
        view = laid.at[chunk].reshape(groups, 4, tiles, LANES)
        return [
            pltpu.make_async_remote_copy(
                src_ref=view.at[:, 1 - bit + 2 * part],
                dst_ref=half_in.at[chunk, part].reshape(groups, tiles, LANES),
                send_sem=half_send.at[chunk, part],
                recv_sem=half_recv.at[chunk, part],
                device_id=(replica + 1 - 2 * bit, tensor),
                device_id_type=MESH,
            )
            for part in range(2)
        ]

    def quarter_copy(chunk):
        return pltpu.make_async_remote_copy(
            src_ref=half.at[chunk, 1 - high],
            dst_ref=quarter_in.at[chunk],
            send_sem=quarter_send.at[chunk],
            recv_sem=quarter_recv.at[chunk],
            device_id=(replica + 2 - 4 * high, tensor),
            device_id_type=MESH,
        )

    def broadcast(slots, size, me, device, send_sem, recv_sem):
        def one(step, carry):
            pltpu.make_async_remote_copy(
                src_ref=slots.at[me],
                dst_ref=slots.at[me],
                send_sem=send_sem,
                recv_sem=recv_sem,
                device_id=device((me + step) % size),
                device_id_type=MESH,
            ).start()
            return carry

        lax.fori_loop(1, size, one, 0)

    def wait_bytes(ref, semaphore):
        pltpu.make_async_copy(ref, ref, semaphore).wait()

    def tile_at(ref, index, step):
        return ref.at[index + (pl.ds(pl.multiple_of(step * tiles, 8), tiles),)]

    def statistics(chunk, pairs_at, slots, me, mine_is_low):
        def one(step, carry):
            for own, theirs in pairs_at(step):
                carry = (
                    carry[0] + own * theirs,
                    carry[1] + own * own,
                    carry[2] + theirs * theirs,
                )
            return carry

        zero = jnp.zeros((tiles, LANES), jnp.float32)
        cross, own, theirs = lax.fori_loop(0, groups, one, (zero, zero, zero))
        lower = jnp.where(mine_is_low, own, theirs)
        upper = jnp.where(mine_is_low, theirs, own)
        message = jnp.zeros((8, LANES), jnp.float32)
        row = 0
        for start, stop in spans(chunk):
            inside = (rows_of_tile >= start) & (rows_of_tile < stop)
            for value in (cross, lower, upper):
                total = jnp.sum(jnp.where(inside, value, 0.0), axis=0, keepdims=True)
                message = jnp.where(tile_row == row, total, message)
                row += 1
        slots[chunk, me] = message

    def weights(chunk, slots, size, mine_is_low):
        total = slots[chunk, 0]
        for index in range(1, size):
            total = total + slots[chunk, index]
        total = jnp.sum(total, axis=1, keepdims=True)
        own_weight = jnp.zeros((tiles, LANES), jnp.float32)
        their_weight = jnp.zeros((tiles, LANES), jnp.float32)
        for number, (start, stop) in enumerate(spans(chunk)):
            inside = (rows_of_tile >= start) & (rows_of_tile < stop)
            cross = total[3 * number : 3 * number + 1]
            low = lower_weight(cross, total[3 * number + 1 : 3 * number + 2])
            up = lower_weight(cross, total[3 * number + 2 : 3 * number + 3])
            own_weight = jnp.where(inside, jnp.where(mine_is_low, low, up), own_weight)
            their_weight = jnp.where(inside, jnp.where(mine_is_low, up, low), their_weight)
        return own_weight, their_weight

    def half_pair(chunk, part, step):
        own = tile_at(laid, (chunk,), step * 4 + bit + 2 * part)[...]
        return own, tile_at(half_in, (chunk, part), step)[...]

    def quarter_pair(chunk, step):
        own = tile_at(half, (chunk, high), step)[...]
        return own, tile_at(quarter_in, (chunk,), step)[...]

    def send_half(chunk):
        for copy in half_copies(chunk):
            copy.start()

    def half_statistics(chunk):
        for copy in half_copies(chunk):
            copy.wait_recv()
        statistics(
            chunk,
            lambda step: [half_pair(chunk, part, step) for part in range(2)],
            stat_pair,
            pair_me,
            bit == 0,
        )
        broadcast(
            stat_pair.at[chunk], pair_size, pair_me, pair_device, pair_send.at[chunk], pair_recv.at[chunk]
        )

    def half_combine(chunk):
        wait_bytes(stat_pair.at[chunk, pl.ds(0, pair_size - 1)], pair_recv.at[chunk])
        own_weight, their_weight = weights(chunk, stat_pair, pair_size, bit == 0)

        def combine(part):
            def one(step, carry):
                own, theirs = half_pair(chunk, part, step)
                tile_at(half, (chunk, part), step)[...] = own_weight * own + their_weight * theirs
                return carry

            lax.fori_loop(0, groups, one, 0)

        combine(1 - high)
        quarter_copy(chunk).start()
        combine(high)

    def quarter_statistics(chunk):
        quarter_copy(chunk).wait_recv()
        statistics(
            chunk,
            lambda step: [quarter_pair(chunk, step)],
            stat_cluster,
            cluster_me,
            high == 0,
        )
        broadcast(
            stat_cluster.at[chunk],
            cluster_size,
            cluster_me,
            cluster_device,
            cluster_send.at[chunk],
            cluster_recv.at[chunk],
        )

    def quarter_combine(chunk):
        wait_bytes(stat_cluster.at[chunk, pl.ds(0, cluster_size - 1)], cluster_recv.at[chunk])
        own_weight, their_weight = weights(chunk, stat_cluster, cluster_size, high == 0)

        def one(step, carry):
            own, theirs = quarter_pair(chunk, step)
            tile_at(quarter, (chunk,), step)[...] = own_weight * own + their_weight * theirs
            return carry

        lax.fori_loop(0, groups, one, 0)

        def send(step, carry):
            other = (group + step) % groups
            pltpu.make_async_remote_copy(
                src_ref=tile_at(quarter, (chunk,), other),
                dst_ref=tile_at(gathered_v, (chunk,), group),
                send_sem=row_send.at[chunk],
                recv_sem=row_recv.at[chunk],
                device_id=group_device(other),
                device_id_type=MESH,
            ).start()
            return carry

        lax.fori_loop(1, groups, send, 0)
        tile_at(gathered_v, (chunk,), group)[...] = tile_at(quarter, (chunk,), group)[...]

    def side_by_side(chunk, start, stop):
        return jnp.concatenate(
            [
                gathered_v[chunk, pl.ds(column, groups, stride=tiles), :]
                for column in range(start, stop)
            ],
            axis=1,
        )

    def gram_first(chunk):
        wait_bytes(gathered_v.at[chunk, pl.ds(0, (groups - 1) * tiles)], row_recv.at[chunk])
        pltpu.make_async_copy(gathered_v.at[chunk], gathered.at[chunk], out_sem.at[chunk]).start()
        grams = []
        for start, stop in spans(chunk):
            vectors = side_by_side(chunk, start, stop)
            grams.append(
                lax.dot_general(
                    vectors,
                    vectors,
                    (((1,), (1,)), ((), ())),
                    precision=lax.Precision.HIGHEST,
                    preferred_element_type=jnp.float32,
                )
            )
        grams.append(jnp.zeros((groups, LANES - groups * len(grams)), jnp.float32))
        gram_rows[chunk, group] = jnp.concatenate(grams, axis=1)
        broadcast(
            gram_rows.at[chunk], groups, group, group_device, gram_row_send.at[chunk], gram_row_recv.at[chunk]
        )

    def gram_second(chunk):
        wait_bytes(gram_rows.at[chunk, pl.ds(0, groups - 1)], gram_row_recv.at[chunk])
        total = gram_rows[chunk, 0]
        for index in range(1, groups):
            total = total + gram_rows[chunk, index]
        gram_cluster[chunk, cluster_me] = total
        broadcast(
            gram_cluster.at[chunk],
            cluster_size,
            cluster_me,
            cluster_device,
            gram_cluster_send.at[chunk],
            gram_cluster_recv.at[chunk],
        )

    def finish(chunk):
        wait_bytes(gram_cluster.at[chunk, pl.ds(0, cluster_size - 1)], gram_cluster_recv.at[chunk])
        total = gram_cluster[chunk, 0]
        for index in range(1, cluster_size):
            total = total + gram_cluster[chunk, index]
        first = sum(len(widths) for widths in members[:chunk])
        worst = jnp.zeros((1, 1), jnp.float32)
        for number, (start, stop) in enumerate(spans(chunk)):
            coefficients, doubtful = tree_weights(total[:, groups * number : groups * (number + 1)])
            vectors = side_by_side(chunk, start, stop)
            outs[first + number][...] = jnp.sum(coefficients * vectors, axis=0, keepdims=True)
            worst = jnp.maximum(worst, jnp.max(doubtful, axis=0, keepdims=True))
        flags[chunk] = jnp.broadcast_to(worst, (8, LANES))

    bring(0)
    pl.semaphore_wait(barrier, cluster_size + groups - 2)
    send_half(0)
    for chunk in range(1, chunks):
        bring(chunk)
        send_half(chunk)
    stages = [
        half_statistics,
        half_combine,
        quarter_statistics,
        quarter_combine,
        gram_first,
        gram_second,
        finish,
    ]
    order = sorted(
        (chunk * 2 + stage, chunk, stage) for chunk in range(chunks) for stage in range(len(stages))
    )
    for _, chunk, stage in order:
        stages[stage](chunk)

    for chunk in range(chunks):
        for copy in half_copies(chunk):
            copy.wait_send()
        quarter_copy(chunk).wait_send()
        wait_bytes(stat_pair.at[chunk, pl.ds(0, pair_size - 1)], pair_send.at[chunk])
        wait_bytes(stat_cluster.at[chunk, pl.ds(0, cluster_size - 1)], cluster_send.at[chunk])
        wait_bytes(gathered_v.at[chunk, pl.ds(0, (groups - 1) * tiles)], row_send.at[chunk])
        wait_bytes(gram_rows.at[chunk, pl.ds(0, groups - 1)], gram_row_send.at[chunk])
        wait_bytes(gram_cluster.at[chunk, pl.ds(0, cluster_size - 1)], gram_cluster_send.at[chunk])
        pltpu.make_async_copy(gathered_v.at[chunk], gathered.at[chunk], out_sem.at[chunk]).wait()


def level_by_level(vectors):
    while vectors.shape[0] > 1:
        lower, upper = vectors[0::2], vectors[1::2]
        totals = lax.psum(
            jnp.stack(
                [
                    jnp.sum(lower * upper, axis=(1, 2)),
                    jnp.sum(lower * lower, axis=(1, 2)),
                    jnp.sum(upper * upper, axis=(1, 2)),
                ]
            ),
            ("replica", "tensor"),
        )
        low = lower_weight(totals[0], totals[1])[:, None, None]
        up = lower_weight(totals[0], totals[2])[:, None, None]
        vectors = low * lower + up * upper
    return vectors.reshape(1, -1)


def per_device(*grads):
    replicas, tensors = lax.axis_size("replica"), lax.axis_size("tensor")
    groups = replicas // 4
    widths = [member.shape[2] // LANES for member in grads]
    tiles = max(widths)
    members = []
    for width in widths:
        if members and sum(members[-1]) + width <= tiles:
            members[-1].append(width)
        else:
            members.append([width])
    chunks = len(members)
    f32 = jnp.float32
    dma = pltpu.SemaphoreType.DMA
    results = pl.pallas_call(
        functools.partial(kernel, replicas, tensors, members, tiles),
        out_shape=[jax.ShapeDtypeStruct((1, member.shape[2]), f32) for member in grads]
        + [
            jax.ShapeDtypeStruct((chunks, groups * tiles, LANES), f32),
            jax.ShapeDtypeStruct((chunks, 8, LANES), f32),
        ],
        in_specs=[pl.BlockSpec(memory_space=pl.ANY)] * len(grads),
        out_specs=[pl.BlockSpec(memory_space=pltpu.VMEM)] * len(grads)
        + [pl.BlockSpec(memory_space=pl.ANY), pl.BlockSpec(memory_space=pltpu.VMEM)],
        scratch_shapes=[
            pltpu.VMEM((chunks, replicas, tiles * LANES), f32),
            pltpu.VMEM((chunks, replicas * tiles, LANES), f32),
            pltpu.VMEM((chunks, 2, groups * tiles, LANES), f32),
            pltpu.VMEM((chunks, 2, groups * tiles, LANES), f32),
            pltpu.VMEM((chunks, groups * tiles, LANES), f32),
            pltpu.VMEM((chunks, groups * tiles, LANES), f32),
            pltpu.VMEM((chunks, 2 * tensors, 8, LANES), f32),
            pltpu.VMEM((chunks, 4 * tensors, 8, LANES), f32),
            pltpu.VMEM((chunks, groups, groups, LANES), f32),
            pltpu.VMEM((chunks, 4 * tensors, groups, LANES), f32),
            pltpu.VMEM((chunks, groups * tiles, LANES), f32),
            dma((len(grads),)),
            dma((chunks, 2)),
            dma((chunks, 2)),
        ]
        + [dma((chunks,))] * 13,
        compiler_params=pltpu.CompilerParams(
            collective_id=0, has_side_effects=True, vmem_limit_bytes=40 * 1024 * 1024
        ),
    )(*grads)
    combined, gathered, flags = results[: len(grads)], results[len(grads)], results[-1]

    def again(combined, gathered):
        outputs = []
        for chunk, in_chunk in enumerate(members):
            vectors = gathered[chunk].reshape(groups, tiles, LANES)
            start = 0
            for width in in_chunk:
                outputs.append(level_by_level(vectors[:, start : start + width]))
                start += width
        return outputs

    return tuple(
        lax.cond(
            jnp.max(flags) > 0.0,
            again,
            lambda combined, gathered: list(combined),
            list(combined),
            gathered,
        )
    )


def solution(mesh):
    return jax.shard_map(
        per_device,
        mesh=mesh,
        in_specs=(P("replica", None, "tensor"),) * 4,
        out_specs=(P("replica", "tensor"),) * 4,
        check_vma=False,
    )
```

time: 889 us -> 169 us (0.19)
  waiting for transfers between devices: 451 us -> 0 us
  starting transfers between devices: 199 us -> 0 us
  Pallas kernels: 0 us -> 160 us
  other arithmetic: 87.1 us -> 0.6 us
  blocking collectives: 83.3 us -> 0 us
  between operations: 61.5 us -> 1.31 us
    ppermute x24 -> x0, waiting for transfers between devices: 451 us -> none  [partner_2(): lax.ppermute(shard, axis, [(i, i ^ 1 << bit) for i in range(lax.axis_size...]
    ppermute x24 -> x0, starting transfers between devices: 199 us -> none  [partner_2(): lax.ppermute(shard, axis, [(i, i ^ 1 << bit) for i in range(lax.axis_size...]
    pallas_call x0 -> x1, Pallas kernels: none -> 160 us  [per_device(): pl.pallas_call(functools.partial(kernel, replicas, tensors, members, tile...]
    psum x6 -> x0, blocking collectives: 83.3 us -> none  [per_device(): totals = lax.psum(statistics, 'tensor')]
    another operation x29 -> x0, other arithmetic: 48.1 us -> none  [per_device(): jnp.stack([pair_statistics(lower_group, upper_group) for lower_group, upp...]
    reduce_sum x23 -> x0, other arithmetic: 28 us -> none  [pair_statistics(): jnp.sum(lower_group * upper_group)]
    add x24 -> x0, other arithmetic: 10.9 us -> none  [combine_pair(): return lower_weight * lower_group + upper_weight * upper_group]
  transfers between devices with their start and end apart: 24 -> 0, of which waited for: 13 -> 0; matrix products, arithmetic and copies ran while one was open for 6% -> 0% of each run, Pallas kernels for 0% -> 0%
where the time goes in v1:
time: 169 us
  Pallas kernels  160 us (95%)
  local copies, waits for them, and re-layouts  6.63 us (4%)
    pallas_call x1, Pallas kernels, per_device(): pl.pallas_call(functools.partial(kernel, replicas, tensors, members, tile...  160 us
    unnamed x12, local copies, waits for them, and re-layouts  6.63 us

profile of v1, /device:TPU:1, one launch (start us, length us, event | category | flops | bytes accessed | tf_op | source)
XLA Modules:
  0.0 168.7 jit_solution(809256265052000355)
XLA Ops:
  0.6 0.0 copy-start
  0.6 1.1 copy-done
  1.8 0.0 copy-start.1
  1.8 1.1 copy-done.1
  2.9 0.0 copy-start.2
  2.9 1.1 copy-done.2
  4.0 0.0 copy-start.3
  4.0 0.9 copy-done.3
  4.9 160.1 %shard_map.83 = (f32[1,2304]{1,0:T(1,128)S(1)}, f32[1,768]{1,0:T(1,128)S(1)}, f32[1,3072]{1,0:T(1,128)S(1)}, f32[1,3072]{1,0:T(1,128)S(1)}, f32[3,384,128]{2,1,0:T(8,128)S(1)}, /*index=5*/f32[3,8,128]{2,1,0:T(8,128)S(1)}) custom-call(f32[1,64,2304]{2,1,0:T(8,128)S(1)} %copy-done.2, f32[1,64,768]{2,1,0:T(8,128)S(1)} %copy-done.3, f32[1,64,3072]{2,1,0:T(8,128)S(1)} %copy-done, ...), custom_call_target="tpu_custom_call" | custom-call | tf_op jit(solution)/shard_map/pallas_call | solution.py:439
  165.0 0.6 reduce_max.9
  166.3 0.6 copy.34
  166.9 0.6 copy.35
  167.5 0.6 copy.36
  168.1 0.6 copy.37
  (1 shorter events, 0.0 us)
Async XLA Ops:
  0.6 1.1 copy-start
  1.8 1.1 copy-start.1
  2.9 1.1 copy-start.2
  4.0 0.9 copy-start.3

commit v2 on v1

--- a/solution.py
+++ b/solution.py
@@ -11,6 +11,10 @@
 LANES = 128
 TRUSTED = 0.03
 MESH = pl.DeviceIdType.MESH
+ORDER = (
+    "s0A s1A b0B s0B b0C r0A t0A s1B c0A s0C r0B t0B s1C c0B r1A t1A r0C t0C c1A c0C r1B t1B c1B "
+    "r2A t2A r1C t1C c1C u2A r2B t2B u2B r2C t2C u2C f2A f2B f2C"
+)
 
 
 def lower_weight(cross, norm):
@@ -60,11 +64,14 @@
     count = sum(len(chunk) for chunk in members)
     chunks = len(members)
     inputs, outs, rest = refs[:count], refs[count : 2 * count], refs[2 * count :]
-    (gathered, flags, raw, laid, half_in, half, quarter_in, quarter,
-     stat_pair, stat_cluster, gram_rows, gram_cluster, gathered_v,
-     in_sem, half_send, half_recv, pair_send, pair_recv, quarter_send, quarter_recv,
-     cluster_send, cluster_recv, row_send, row_recv, gram_row_send, gram_row_recv,
-     gram_cluster_send, gram_cluster_recv, out_sem) = rest
+    (gathered, flag, raw, laid, half_in, half, quarter_in, quarter, gathered_v, doubts,
+     half_shares, half_totals, quarter_shares, quarter_totals, gram_shares, gram_parts, gram_totals,
+     in_sem, half_send, half_recv, *semaphores) = rest
+    (quarter_send, quarter_recv, row_send, row_recv, out_sem,
+     half_share_send, half_share_recv, half_total_send, half_total_recv,
+     quarter_share_send, quarter_share_recv, quarter_total_send, quarter_total_recv,
+     gram_share_send, gram_share_recv, gram_part_send, gram_part_recv,
+     gram_total_send, gram_total_recv) = semaphores
 
     groups = replicas // 4
     replica = lax.axis_index("replica")
@@ -73,15 +80,15 @@
     local = replica % 4
     bit = local % 2
     high = local // 2
-    pair_size, cluster_size = 2 * tensors, 4 * tensors
-    pair_me = bit * tensors + tensor
-    cluster_me = local * tensors + tensor
+
+    def tensor_device(index):
+        return (replica, index)
 
     def pair_device(index):
-        return (group * 4 + high * 2 + index // tensors, index % tensors)
-
-    def cluster_device(index):
-        return (group * 4 + index // tensors, index % tensors)
+        return (group * 4 + high * 2 + index, tensor)
+
+    def local_device(index):
+        return (group * 4 + index, tensor)
 
     def group_device(index):
         return (index * 4 + local, tensor)
@@ -97,7 +104,8 @@
 
         lax.fori_loop(1, size, one, 0)
 
-    greet(cluster_size, cluster_me, cluster_device)
+    greet(tensors, tensor, tensor_device)
+    greet(4, local, local_device)
     greet(groups, group, group_device)
 
     input_copies = []
@@ -141,19 +149,15 @@
 
         lax.fori_loop(0, replicas // 8, block, 0)
 
-    def half_copies(chunk):
-        view = laid.at[chunk].reshape(groups, 4, tiles, LANES)
-        return [
-            pltpu.make_async_remote_copy(
-                src_ref=view.at[:, 1 - bit + 2 * part],
-                dst_ref=half_in.at[chunk, part].reshape(groups, tiles, LANES),
-                send_sem=half_send.at[chunk, part],
-                recv_sem=half_recv.at[chunk, part],
-                device_id=(replica + 1 - 2 * bit, tensor),
-                device_id_type=MESH,
-            )
-            for part in range(2)
-        ]
+    def half_copy(part, chunk):
+        return pltpu.make_async_remote_copy(
+            src_ref=laid.at[chunk].reshape(groups, 4, tiles, LANES).at[:, 1 - bit + 2 * part],
+            dst_ref=half_in.at[chunk, part].reshape(groups, tiles, LANES),
+            send_sem=half_send.at[chunk, part],
+            recv_sem=half_recv.at[chunk, part],
+            device_id=(replica + 1 - 2 * bit, tensor),
+            device_id_type=MESH,
+        )
 
     def quarter_copy(chunk):
         return pltpu.make_async_remote_copy(
@@ -165,13 +169,13 @@
             device_id_type=MESH,
         )
 
-    def broadcast(slots, size, me, device, send_sem, recv_sem):
+    def broadcast(chunk, slots, size, me, device, send_sem, recv_sem):
         def one(step, carry):
             pltpu.make_async_remote_copy(
-                src_ref=slots.at[me],
-                dst_ref=slots.at[me],
-                send_sem=send_sem,
-                recv_sem=recv_sem,
+                src_ref=slots.at[chunk, me],
+                dst_ref=slots.at[chunk, me],
+                send_sem=send_sem.at[chunk],
+                recv_sem=recv_sem.at[chunk],
                 device_id=device((me + step) % size),
                 device_id_type=MESH,
             ).start()
@@ -182,10 +186,17 @@
     def wait_bytes(ref, semaphore):
         pltpu.make_async_copy(ref, ref, semaphore).wait()
 
+    def collect(chunk, slots, size, recv_sem):
+        wait_bytes(slots.at[chunk, pl.ds(0, size - 1)], recv_sem.at[chunk])
+        total = slots[chunk, 0]
+        for index in range(1, size):
+            total = total + slots[chunk, index]
+        return total
+
     def tile_at(ref, index, step):
         return ref.at[index + (pl.ds(pl.multiple_of(step * tiles, 8), tiles),)]
 
-    def statistics(chunk, pairs_at, slots, me, mine_is_low):
+    def statistics(chunk, pairs_at, mine_is_low):
         def one(step, carry):
             for own, theirs in pairs_at(step):
                 carry = (
@@ -207,12 +218,9 @@
                 total = jnp.sum(jnp.where(inside, value, 0.0), axis=0, keepdims=True)
                 message = jnp.where(tile_row == row, total, message)
                 row += 1
-        slots[chunk, me] = message
-
-    def weights(chunk, slots, size, mine_is_low):
-        total = slots[chunk, 0]
-        for index in range(1, size):
-            total = total + slots[chunk, index]
+        return message
+
+    def weights(chunk, total, mine_is_low):
         total = jnp.sum(total, axis=1, keepdims=True)
         own_weight = jnp.zeros((tiles, LANES), jnp.float32)
         their_weight = jnp.zeros((tiles, LANES), jnp.float32)
@@ -233,27 +241,24 @@
         own = tile_at(half, (chunk, high), step)[...]
         return own, tile_at(quarter_in, (chunk,), step)[...]
 
-    def send_half(chunk):
-        for copy in half_copies(chunk):
-            copy.start()
-
-    def half_statistics(chunk):
-        for copy in half_copies(chunk):
-            copy.wait_recv()
-        statistics(
-            chunk,
-            lambda step: [half_pair(chunk, part, step) for part in range(2)],
-            stat_pair,
-            pair_me,
-            bit == 0,
-        )
-        broadcast(
-            stat_pair.at[chunk], pair_size, pair_me, pair_device, pair_send.at[chunk], pair_recv.at[chunk]
-        )
+    def send_half(part, chunk):
+        half_copy(part, chunk).start()
+
+    def half_share(chunk):
+        for part in range(2):
+            half_copy(part, chunk).wait_recv()
+        half_shares[chunk, tensor] = statistics(
+            chunk, lambda step: [half_pair(chunk, part, step) for part in range(2)], bit == 0
+        )
+        broadcast(chunk, half_shares, tensors, tensor, tensor_device, half_share_send, half_share_recv)
+
+    def half_total(chunk):
+        half_totals[chunk, bit] = collect(chunk, half_shares, tensors, half_share_recv)
+        broadcast(chunk, half_totals, 2, bit, pair_device, half_total_send, half_total_recv)
 
     def half_combine(chunk):
-        wait_bytes(stat_pair.at[chunk, pl.ds(0, pair_size - 1)], pair_recv.at[chunk])
-        own_weight, their_weight = weights(chunk, stat_pair, pair_size, bit == 0)
+        total = collect(chunk, half_totals, 2, half_total_recv)
+        own_weight, their_weight = weights(chunk, total, bit == 0)
 
         def combine(part):
             def one(step, carry):
@@ -267,27 +272,22 @@
         quarter_copy(chunk).start()
         combine(high)
 
-    def quarter_statistics(chunk):
+    def quarter_share(chunk):
         quarter_copy(chunk).wait_recv()
-        statistics(
-            chunk,
-            lambda step: [quarter_pair(chunk, step)],
-            stat_cluster,
-            cluster_me,
-            high == 0,
+        quarter_shares[chunk, tensor] = statistics(
+            chunk, lambda step: [quarter_pair(chunk, step)], high == 0
         )
         broadcast(
-            stat_cluster.at[chunk],
-            cluster_size,
-            cluster_me,
-            cluster_device,
-            cluster_send.at[chunk],
-            cluster_recv.at[chunk],
-        )
+            chunk, quarter_shares, tensors, tensor, tensor_device, quarter_share_send, quarter_share_recv
+        )
+
+    def quarter_total(chunk):
+        quarter_totals[chunk, local] = collect(chunk, quarter_shares, tensors, quarter_share_recv)
+        broadcast(chunk, quarter_totals, 4, local, local_device, quarter_total_send, quarter_total_recv)
 
     def quarter_combine(chunk):
-        wait_bytes(stat_cluster.at[chunk, pl.ds(0, cluster_size - 1)], cluster_recv.at[chunk])
-        own_weight, their_weight = weights(chunk, stat_cluster, cluster_size, high == 0)
+        total = collect(chunk, quarter_totals, 4, quarter_total_recv)
+        own_weight, their_weight = weights(chunk, total, high == 0)
 
         def one(step, carry):
             own, theirs = quarter_pair(chunk, step)
@@ -320,86 +320,91 @@
             axis=1,
         )
 
-    def gram_first(chunk):
+    def gram_share(chunk):
         wait_bytes(gathered_v.at[chunk, pl.ds(0, (groups - 1) * tiles)], row_recv.at[chunk])
         pltpu.make_async_copy(gathered_v.at[chunk], gathered.at[chunk], out_sem.at[chunk]).start()
-        grams = []
+        pieces = []
         for start, stop in spans(chunk):
             vectors = side_by_side(chunk, start, stop)
-            grams.append(
-                lax.dot_general(
-                    vectors,
-                    vectors,
-                    (((1,), (1,)), ((), ())),
-                    precision=lax.Precision.HIGHEST,
-                    preferred_element_type=jnp.float32,
-                )
+            gram = lax.dot_general(
+                vectors,
+                vectors,
+                (((1,), (1,)), ((), ())),
+                precision=lax.Precision.HIGHEST,
+                preferred_element_type=jnp.float32,
             )
-        grams.append(jnp.zeros((groups, LANES - groups * len(grams)), jnp.float32))
-        gram_rows[chunk, group] = jnp.concatenate(grams, axis=1)
-        broadcast(
-            gram_rows.at[chunk], groups, group, group_device, gram_row_send.at[chunk], gram_row_recv.at[chunk]
-        )
-
-    def gram_second(chunk):
-        wait_bytes(gram_rows.at[chunk, pl.ds(0, groups - 1)], gram_row_recv.at[chunk])
-        total = gram_rows[chunk, 0]
-        for index in range(1, groups):
-            total = total + gram_rows[chunk, index]
-        gram_cluster[chunk, cluster_me] = total
-        broadcast(
-            gram_cluster.at[chunk],
-            cluster_size,
-            cluster_me,
-            cluster_device,
-            gram_cluster_send.at[chunk],
-            gram_cluster_recv.at[chunk],
-        )
+            pieces += [gram[top : top + 8] for top in range(0, groups, 8)]
+        pieces.append(jnp.zeros((8, LANES - groups * len(pieces)), jnp.float32))
+        gram_shares[chunk, tensor] = jnp.concatenate(pieces, axis=1)
+        broadcast(chunk, gram_shares, tensors, tensor, tensor_device, gram_share_send, gram_share_recv)
+
+    def gram_part(chunk):
+        gram_parts[chunk, local] = collect(chunk, gram_shares, tensors, gram_share_recv)
+        broadcast(chunk, gram_parts, 4, local, local_device, gram_part_send, gram_part_recv)
+
+    def gram_total(chunk):
+        gram_totals[chunk, group] = collect(chunk, gram_parts, 4, gram_part_recv)
+        broadcast(chunk, gram_totals, groups, group, group_device, gram_total_send, gram_total_recv)
 
     def finish(chunk):
-        wait_bytes(gram_cluster.at[chunk, pl.ds(0, cluster_size - 1)], gram_cluster_recv.at[chunk])
-        total = gram_cluster[chunk, 0]
-        for index in range(1, cluster_size):
-            total = total + gram_cluster[chunk, index]
+        total = collect(chunk, gram_totals, groups, gram_total_recv)
         first = sum(len(widths) for widths in members[:chunk])
         worst = jnp.zeros((1, 1), jnp.float32)
+        blocks = groups // 8
         for number, (start, stop) in enumerate(spans(chunk)):
-            coefficients, doubtful = tree_weights(total[:, groups * number : groups * (number + 1)])
+            gram = jnp.concatenate(
+                [
+                    total[:, groups * block : groups * (block + 1)]
+                    for block in range(number * blocks, (number + 1) * blocks)
+                ],
+                axis=0,
+            )
+            coefficients, doubtful = tree_weights(gram)
             vectors = side_by_side(chunk, start, stop)
             outs[first + number][...] = jnp.sum(coefficients * vectors, axis=0, keepdims=True)
             worst = jnp.maximum(worst, jnp.max(doubtful, axis=0, keepdims=True))
-        flags[chunk] = jnp.broadcast_to(worst, (8, LANES))
+        doubts[chunk] = jnp.broadcast_to(worst, (8, LANES))
 
     bring(0)
-    pl.semaphore_wait(barrier, cluster_size + groups - 2)
-    send_half(0)
+    pl.semaphore_wait(barrier, tensors + 4 + groups - 3)
+    steps = {
+        "s0": functools.partial(send_half, 0),
+        "s1": functools.partial(send_half, 1),
+        "b0": bring,
+        "r0": half_share,
+        "t0": half_total,
+        "c0": half_combine,
+        "r1": quarter_share,
+        "t1": quarter_total,
+        "c1": quarter_combine,
+        "r2": gram_share,
+        "t2": gram_part,
+        "u2": gram_total,
+        "f2": finish,
+    }
+    for step in ORDER.split():
+        steps[step[:2]]("ABC".index(step[2]))
+
+    worst = doubts[0]
     for chunk in range(1, chunks):
-        bring(chunk)
-        send_half(chunk)
-    stages = [
-        half_statistics,
-        half_combine,
-        quarter_statistics,
-        quarter_combine,
-        gram_first,
-        gram_second,
-        finish,
-    ]
-    order = sorted(
-        (chunk * 2 + stage, chunk, stage) for chunk in range(chunks) for stage in range(len(stages))
-    )
-    for _, chunk, stage in order:
-        stages[stage](chunk)
+        worst = jnp.maximum(worst, doubts[chunk])
+    flag[0] = jnp.max(worst)
 
     for chunk in range(chunks):
-        for copy in half_copies(chunk):
-            copy.wait_send()
+        for part in range(2):
+            half_copy(part, chunk).wait_send()
         quarter_copy(chunk).wait_send()
-        wait_bytes(stat_pair.at[chunk, pl.ds(0, pair_size - 1)], pair_send.at[chunk])
-        wait_bytes(stat_cluster.at[chunk, pl.ds(0, cluster_size - 1)], cluster_send.at[chunk])
         wait_bytes(gathered_v.at[chunk, pl.ds(0, (groups - 1) * tiles)], row_send.at[chunk])
-        wait_bytes(gram_rows.at[chunk, pl.ds(0, groups - 1)], gram_row_send.at[chunk])
-        wait_bytes(gram_cluster.at[chunk, pl.ds(0, cluster_size - 1)], gram_cluster_send.at[chunk])
+        for slots, size, sent in (
+            (half_shares, tensors, half_share_send),
+            (half_totals, 2, half_total_send),
+            (quarter_shares, tensors, quarter_share_send),
+            (quarter_totals, 4, quarter_total_send),
+            (gram_shares, tensors, gram_share_send),
+            (gram_parts, 4, gram_part_send),
+            (gram_totals, groups, gram_total_send),
+        ):
+            wait_bytes(slots.at[chunk, pl.ds(0, size - 1)], sent.at[chunk])
         pltpu.make_async_copy(gathered_v.at[chunk], gathered.at[chunk], out_sem.at[chunk]).wait()
 
 
@@ -441,11 +446,11 @@
         out_shape=[jax.ShapeDtypeStruct((1, member.shape[2]), f32) for member in grads]
         + [
             jax.ShapeDtypeStruct((chunks, groups * tiles, LANES), f32),
-            jax.ShapeDtypeStruct((chunks, 8, LANES), f32),
+            jax.ShapeDtypeStruct((1,), f32),
         ],
         in_specs=[pl.BlockSpec(memory_space=pl.ANY)] * len(grads),
         out_specs=[pl.BlockSpec(memory_space=pltpu.VMEM)] * len(grads)
-        + [pl.BlockSpec(memory_space=pl.ANY), pl.BlockSpec(memory_space=pltpu.VMEM)],
+        + [pl.BlockSpec(memory_space=pl.ANY), pl.BlockSpec(memory_space=pltpu.SMEM)],
         scratch_shapes=[
             pltpu.VMEM((chunks, replicas, tiles * LANES), f32),
             pltpu.VMEM((chunks, replicas * tiles, LANES), f32),
@@ -453,21 +458,24 @@
             pltpu.VMEM((chunks, 2, groups * tiles, LANES), f32),
             pltpu.VMEM((chunks, groups * tiles, LANES), f32),
             pltpu.VMEM((chunks, groups * tiles, LANES), f32),
-            pltpu.VMEM((chunks, 2 * tensors, 8, LANES), f32),
-            pltpu.VMEM((chunks, 4 * tensors, 8, LANES), f32),
-            pltpu.VMEM((chunks, groups, groups, LANES), f32),
-            pltpu.VMEM((chunks, 4 * tensors, groups, LANES), f32),
             pltpu.VMEM((chunks, groups * tiles, LANES), f32),
+            pltpu.VMEM((chunks, 8, LANES), f32),
+        ]
+        + [
+            pltpu.VMEM((chunks, size, 8, LANES), f32)
+            for size in (tensors, 2, tensors, 4, tensors, 4, groups)
+        ]
+        + [
             dma((len(grads),)),
             dma((chunks, 2)),
             dma((chunks, 2)),
         ]
-        + [dma((chunks,))] * 13,
+        + [dma((chunks,))] * 19,
         compiler_params=pltpu.CompilerParams(
-            collective_id=0, has_side_effects=True, vmem_limit_bytes=40 * 1024 * 1024
+            collective_id=0, has_side_effects=True, vmem_limit_bytes=60 * 1024 * 1024
         ),
     )(*grads)
-    combined, gathered, flags = results[: len(grads)], results[len(grads)], results[-1]
+    combined, gathered, flag = results[: len(grads)], results[len(grads)], results[-1]
 
     def again(combined, gathered):
         outputs = []
@@ -481,7 +489,7 @@
 
     return tuple(
         lax.cond(
-            jnp.max(flags) > 0.0,
+            flag[0] > 0.0,
             again,
             lambda combined, gathered: list(combined),
             list(combined),

time: 169 us -> 128 us (0.76)
  Pallas kernels: 160 us -> 125 us
  local copies, waits for them, and re-layouts: 6.63 us -> 2.38 us
    pallas_call x1, Pallas kernels: 160 us -> 125 us  [per_device(): pl.pallas_call(functools.partial(kernel, replicas, tensors, members, tile...]
    unnamed x12 -> x4, local copies, waits for them, and re-layouts: 6.63 us -> 2.38 us
where the time goes in v2:
time: 128 us
  Pallas kernels  125 us (98%)
  local copies, waits for them, and re-layouts  2.38 us (2%)
  between operations  1.34 us (1%)
    pallas_call x1, Pallas kernels, per_device(): pl.pallas_call(functools.partial(kernel, replicas, tensors, members, tile...  125 us

profile of v2, /device:TPU:1, one launch (start us, length us, event | category | flops | bytes accessed | tf_op | source)
XLA Modules:
  0.0 128.3 jit_solution(18066639783311764754)
XLA Ops:
  0.6 124.6 %shard_map.83 = (f32[1,2304]{1,0:T(1,128)S(1)}, f32[1,768]{1,0:T(1,128)S(1)}, f32[1,3072]{1,0:T(1,128)S(1)}, f32[1,3072]{1,0:T(1,128)S(1)}, f32[3,384,128]{2,1,0:T(8,128)S(1)}, /*index=5*/f32[1]{0:T(128)}) custom-call(f32[1,64,2304]{2,1,0:T(8,128)} %refs_0_.1, f32[1,64,768]{2,1,0:T(8,128)} %refs_1_.1, f32[1,64,3072]{2,1,0:T(8,128)} %refs_2_.1, ...), custom_call_target="tpu_custom_call" | custom-call | tf_op jit(solution)/shard_map/pallas_call | solution.py:444
  125.9 0.6 copy.34
  126.5 0.6 copy.35
  127.1 0.6 copy.36
  127.7 0.6 copy.37
  (1 shorter events, 0.0 us)

commit v3 on v2

--- a/solution.py
+++ b/solution.py
@@ -12,8 +12,9 @@
 TRUSTED = 0.03
 MESH = pl.DeviceIdType.MESH
 ORDER = (
-    "s0A s1A b0B s0B b0C r0A t0A s1B c0A s0C r0B t0B s1C c0B r1A t1A r0C t0C c1A c0C r1B t1B c1B "
-    "r2A t2A r1C t1C c1C u2A r2B t2B u2B r2C t2C u2C f2A f2B f2C"
+    "s0A", "s1A", "b0B", "s0B", "b0C", "r0A", "s1B", "c0A", "q1A", "r0B", "s0C", "s1C", "r1A",
+    "c0B", "q1B", "r0C", "c1A", "r1B", "c0C", "w1A", "q1C", "c1B", "r1C", "w1B", "c1C", "w1C",
+    "r2A", "r2B", "r2C", "g2C", "u2C", "f2C",
 )
 
 
@@ -64,14 +65,12 @@
     count = sum(len(chunk) for chunk in members)
     chunks = len(members)
     inputs, outs, rest = refs[:count], refs[count : 2 * count], refs[2 * count :]
-    (gathered, flag, raw, laid, half_in, half, quarter_in, quarter, gathered_v, doubts,
-     half_shares, half_totals, quarter_shares, quarter_totals, gram_shares, gram_parts, gram_totals,
+    (gathered, flag, raw, laid, half_in, half, quarter_in, quarter, gathered_v, grams,
+     half_sums, quarter_sums, gram_parts, gram_totals,
      in_sem, half_send, half_recv, *semaphores) = rest
     (quarter_send, quarter_recv, row_send, row_recv, out_sem,
-     half_share_send, half_share_recv, half_total_send, half_total_recv,
-     quarter_share_send, quarter_share_recv, quarter_total_send, quarter_total_recv,
-     gram_share_send, gram_share_recv, gram_part_send, gram_part_recv,
-     gram_total_send, gram_total_recv) = semaphores
+     half_sum_send, half_sum_recv, quarter_sum_send, quarter_sum_recv,
+     gram_part_send, gram_part_recv, gram_total_send, gram_total_recv) = semaphores
 
     groups = replicas // 4
     replica = lax.axis_index("replica")
@@ -81,14 +80,14 @@
     bit = local % 2
     high = local // 2
 
-    def tensor_device(index):
-        return (replica, index)
+    pair_me, cluster_me = bit * tensors + tensor, local * tensors + tensor
+    pair_size, cluster_size = 2 * tensors, 4 * tensors
 
     def pair_device(index):
-        return (group * 4 + high * 2 + index, tensor)
-
-    def local_device(index):
-        return (group * 4 + index, tensor)
+        return (group * 4 + high * 2 + index // tensors, index % tensors)
+
+    def cluster_device(index):
+        return (group * 4 + index // tensors, index % tensors)
 
     def group_device(index):
         return (index * 4 + local, tensor)
@@ -104,8 +103,7 @@
 
         lax.fori_loop(1, size, one, 0)
 
-    greet(tensors, tensor, tensor_device)
-    greet(4, local, local_device)
+    greet(cluster_size, cluster_me, cluster_device)
     greet(groups, group, group_device)
 
     input_copies = []
@@ -126,7 +124,7 @@
         copy.start()
 
     rows_of_tile = lax.broadcasted_iota(jnp.int32, (tiles, LANES), 0)
-    tile_row = lax.broadcasted_iota(jnp.int32, (8, LANES), 0)
+    lane = lax.broadcasted_iota(jnp.int32, (1, LANES), 1)
 
     def spans(chunk):
         start = 0
@@ -159,12 +157,13 @@
             device_id_type=MESH,
         )
 
-    def quarter_copy(chunk):
+    def quarter_copy(part, chunk):
+        rows = pl.ds(part * (groups // 2) * tiles, groups // 2 * tiles)
         return pltpu.make_async_remote_copy(
-            src_ref=half.at[chunk, 1 - high],
-            dst_ref=quarter_in.at[chunk],
-            send_sem=quarter_send.at[chunk],
-            recv_sem=quarter_recv.at[chunk],
+            src_ref=half.at[chunk, 1 - high, rows],
+            dst_ref=quarter_in.at[chunk, rows],
+            send_sem=quarter_send.at[chunk, part],
+            recv_sem=quarter_recv.at[chunk, part],
             device_id=(replica + 2 - 4 * high, tensor),
             device_id_type=MESH,
         )
@@ -210,25 +209,27 @@
         cross, own, theirs = lax.fori_loop(0, groups, one, (zero, zero, zero))
         lower = jnp.where(mine_is_low, own, theirs)
         upper = jnp.where(mine_is_low, theirs, own)
-        message = jnp.zeros((8, LANES), jnp.float32)
-        row = 0
+        message = jnp.zeros((1, LANES), jnp.float32)
+        place = 0
         for start, stop in spans(chunk):
             inside = (rows_of_tile >= start) & (rows_of_tile < stop)
             for value in (cross, lower, upper):
                 total = jnp.sum(jnp.where(inside, value, 0.0), axis=0, keepdims=True)
-                message = jnp.where(tile_row == row, total, message)
-                row += 1
+                total = jnp.sum(total, axis=1, keepdims=True)
+                message = jnp.where(lane == place, total, message)
+                place += 1
         return message
 
     def weights(chunk, total, mine_is_low):
-        total = jnp.sum(total, axis=1, keepdims=True)
         own_weight = jnp.zeros((tiles, LANES), jnp.float32)
         their_weight = jnp.zeros((tiles, LANES), jnp.float32)
         for number, (start, stop) in enumerate(spans(chunk)):
             inside = (rows_of_tile >= start) & (rows_of_tile < stop)
-            cross = total[3 * number : 3 * number + 1]
-            low = lower_weight(cross, total[3 * number + 1 : 3 * number + 2])
-            up = lower_weight(cross, total[3 * number + 2 : 3 * number + 3])
+            cross, low_norm, up_norm = (
+                total[:, 3 * number + place : 3 * number + place + 1] for place in range(3)
+            )
+            low = lower_weight(cross, low_norm)
+            up = lower_weight(cross, up_norm)
             own_weight = jnp.where(inside, jnp.where(mine_is_low, low, up), own_weight)
             their_weight = jnp.where(inside, jnp.where(mine_is_low, up, low), their_weight)
         return own_weight, their_weight
@@ -241,63 +242,61 @@
         own = tile_at(half, (chunk, high), step)[...]
         return own, tile_at(quarter_in, (chunk,), step)[...]
 
+    kept, others = {}, {}
+
     def send_half(part, chunk):
         half_copy(part, chunk).start()
 
-    def half_share(chunk):
+    def half_sum(chunk):
         for part in range(2):
             half_copy(part, chunk).wait_recv()
-        half_shares[chunk, tensor] = statistics(
+        half_sums[chunk, pair_me] = statistics(
             chunk, lambda step: [half_pair(chunk, part, step) for part in range(2)], bit == 0
         )
-        broadcast(chunk, half_shares, tensors, tensor, tensor_device, half_share_send, half_share_recv)
-
-    def half_total(chunk):
-        half_totals[chunk, bit] = collect(chunk, half_shares, tensors, half_share_recv)
-        broadcast(chunk, half_totals, 2, bit, pair_device, half_total_send, half_total_recv)
+        broadcast(chunk, half_sums, pair_size, pair_me, pair_device, half_sum_send, half_sum_recv)
 
     def half_combine(chunk):
-        total = collect(chunk, half_totals, 2, half_total_recv)
+        total = collect(chunk, half_sums, pair_size, half_sum_recv)
         own_weight, their_weight = weights(chunk, total, bit == 0)
 
-        def combine(part):
+        def combine(part, start, stop):
             def one(step, carry):
                 own, theirs = half_pair(chunk, part, step)
                 tile_at(half, (chunk, part), step)[...] = own_weight * own + their_weight * theirs
                 return carry
 
-            lax.fori_loop(0, groups, one, 0)
-
-        combine(1 - high)
-        quarter_copy(chunk).start()
-        combine(high)
-
-    def quarter_share(chunk):
-        quarter_copy(chunk).wait_recv()
-        quarter_shares[chunk, tensor] = statistics(
+            lax.fori_loop(start, stop, one, 0)
+
+        combine(1 - high, 0, groups // 2)
+        quarter_copy(0, chunk).start()
+        combine(1 - high, groups // 2, groups)
+        kept[chunk] = lambda: combine(high, 0, groups)
+
+    def send_quarter(chunk):
+        quarter_copy(1, chunk).start()
+        kept[chunk]()
+
+    def quarter_sum(chunk):
+        for part in range(2):
+            quarter_copy(part, chunk).wait_recv()
+        quarter_sums[chunk, cluster_me] = statistics(
             chunk, lambda step: [quarter_pair(chunk, step)], high == 0
         )
         broadcast(
-            chunk, quarter_shares, tensors, tensor, tensor_device, quarter_share_send, quarter_share_recv
-        )
-
-    def quarter_total(chunk):
-        quarter_totals[chunk, local] = collect(chunk, quarter_shares, tensors, quarter_share_recv)
-        broadcast(chunk, quarter_totals, 4, local, local_device, quarter_total_send, quarter_total_recv)
+            chunk, quarter_sums, cluster_size, cluster_me, cluster_device, quarter_sum_send, quarter_sum_recv
+        )
 
     def quarter_combine(chunk):
-        total = collect(chunk, quarter_totals, 4, quarter_total_recv)
+        total = collect(chunk, quarter_sums, cluster_size, quarter_sum_recv)
         own_weight, their_weight = weights(chunk, total, high == 0)
 
-        def one(step, carry):
-            own, theirs = quarter_pair(chunk, step)
-            tile_at(quarter, (chunk,), step)[...] = own_weight * own + their_weight * theirs
-            return carry
-
-        lax.fori_loop(0, groups, one, 0)
+        def combined(index):
+            own, theirs = quarter_pair(chunk, index)
+            return own_weight * own + their_weight * theirs
 
         def send(step, carry):
             other = (group + step) % groups
+            tile_at(quarter, (chunk,), other)[...] = combined(other)
             pltpu.make_async_remote_copy(
                 src_ref=tile_at(quarter, (chunk,), other),
                 dst_ref=tile_at(gathered_v, (chunk,), group),
@@ -308,8 +307,16 @@
             ).start()
             return carry
 
-        lax.fori_loop(1, groups, send, 0)
-        tile_at(gathered_v, (chunk,), group)[...] = tile_at(quarter, (chunk,), group)[...]
+        lax.fori_loop(1, groups // 2 + 1, send, 0)
+
+        def rest():
+            lax.fori_loop(groups // 2 + 1, groups, send, 0)
+            tile_at(gathered_v, (chunk,), group)[...] = combined(group)
+
+        others[chunk] = rest
+
+    def send_rows(chunk):
+        others[chunk]()
 
     def side_by_side(chunk, start, stop):
         return jnp.concatenate(
@@ -320,10 +327,13 @@
             axis=1,
         )
 
-    def gram_share(chunk):
+    blocks = groups // 8
+
+    def gram_of(chunk):
         wait_bytes(gathered_v.at[chunk, pl.ds(0, (groups - 1) * tiles)], row_recv.at[chunk])
         pltpu.make_async_copy(gathered_v.at[chunk], gathered.at[chunk], out_sem.at[chunk]).start()
-        pieces = []
+        first = sum(len(widths) for widths in members[:chunk])
+        pieces = [jnp.zeros((8, first * groups * blocks), jnp.float32)] if first else []
         for start, stop in spans(chunk):
             vectors = side_by_side(chunk, start, stop)
             gram = lax.dot_general(
@@ -334,78 +344,81 @@
                 preferred_element_type=jnp.float32,
             )
             pieces += [gram[top : top + 8] for top in range(0, groups, 8)]
-        pieces.append(jnp.zeros((8, LANES - groups * len(pieces)), jnp.float32))
-        gram_shares[chunk, tensor] = jnp.concatenate(pieces, axis=1)
-        broadcast(chunk, gram_shares, tensors, tensor, tensor_device, gram_share_send, gram_share_recv)
-
-    def gram_part(chunk):
-        gram_parts[chunk, local] = collect(chunk, gram_shares, tensors, gram_share_recv)
-        broadcast(chunk, gram_parts, 4, local, local_device, gram_part_send, gram_part_recv)
-
-    def gram_total(chunk):
-        gram_totals[chunk, group] = collect(chunk, gram_parts, 4, gram_part_recv)
-        broadcast(chunk, gram_totals, groups, group, group_device, gram_total_send, gram_total_recv)
-
-    def finish(chunk):
-        total = collect(chunk, gram_totals, groups, gram_total_recv)
-        first = sum(len(widths) for widths in members[:chunk])
+        used = sum(piece.shape[1] for piece in pieces)
+        if used < LANES:
+            pieces.append(jnp.zeros((8, LANES - used), jnp.float32))
+        grams[chunk] = jnp.concatenate(pieces, axis=1)
+
+    def gram_part(_):
+        total = grams[0]
+        for chunk in range(1, chunks):
+            total = total + grams[chunk]
+        gram_parts[0, cluster_me] = total
+        broadcast(
+            0, gram_parts, cluster_size, cluster_me, cluster_device, gram_part_send, gram_part_recv
+        )
+
+    def gram_total(_):
+        gram_totals[0, group] = collect(0, gram_parts, cluster_size, gram_part_recv)
+        broadcast(0, gram_totals, groups, group, group_device, gram_total_send, gram_total_recv)
+
+    def finish(_):
+        total = collect(0, gram_totals, groups, gram_total_recv)
         worst = jnp.zeros((1, 1), jnp.float32)
-        blocks = groups // 8
-        for number, (start, stop) in enumerate(spans(chunk)):
-            gram = jnp.concatenate(
-                [
-                    total[:, groups * block : groups * (block + 1)]
-                    for block in range(number * blocks, (number + 1) * blocks)
-                ],
-                axis=0,
-            )
-            coefficients, doubtful = tree_weights(gram)
-            vectors = side_by_side(chunk, start, stop)
-            outs[first + number][...] = jnp.sum(coefficients * vectors, axis=0, keepdims=True)
-            worst = jnp.maximum(worst, jnp.max(doubtful, axis=0, keepdims=True))
-        doubts[chunk] = jnp.broadcast_to(worst, (8, LANES))
+        number = 0
+        for chunk in range(chunks):
+            for start, stop in spans(chunk):
+                gram = jnp.concatenate(
+                    [
+                        total[:, groups * block : groups * (block + 1)]
+                        for block in range(number * blocks, (number + 1) * blocks)
+                    ],
+                    axis=0,
+                )
+                coefficients, doubtful = tree_weights(gram)
+                vectors = side_by_side(chunk, start, stop)
+                outs[number][...] = jnp.sum(coefficients * vectors, axis=0, keepdims=True)
+                worst = jnp.maximum(worst, jnp.max(doubtful, axis=0, keepdims=True))
+                number += 1
+        flag[0] = worst[0, 0]
 
     bring(0)
-    pl.semaphore_wait(barrier, tensors + 4 + groups - 3)
+    pl.semaphore_wait(barrier, cluster_size + groups - 2)
     steps = {
         "s0": functools.partial(send_half, 0),
         "s1": functools.partial(send_half, 1),
         "b0": bring,
-        "r0": half_share,
-        "t0": half_total,
+        "r0": half_sum,
         "c0": half_combine,
-        "r1": quarter_share,
-        "t1": quarter_total,
+        "q1": send_quarter,
+        "r1": quarter_sum,
         "c1": quarter_combine,
-        "r2": gram_share,
-        "t2": gram_part,
+        "w1": send_rows,
+        "r2": gram_of,
+        "g2": gram_part,
         "u2": gram_total,
         "f2": finish,
     }
-    for step in ORDER.split():
+    for step in ORDER:
         steps[step[:2]]("ABC".index(step[2]))
-
-    worst = doubts[0]
-    for chunk in range(1, chunks):
-        worst = jnp.maximum(worst, doubts[chunk])
-    flag[0] = jnp.max(worst)
 
     for chunk in range(chunks):
         for part in range(2):
             half_copy(part, chunk).wait_send()
-        quarter_copy(chunk).wait_send()
+        for part in range(2):
+            quarter_copy(part, chunk).wait_send()
         wait_bytes(gathered_v.at[chunk, pl.ds(0, (groups - 1) * tiles)], row_send.at[chunk])
         for slots, size, sent in (
-            (half_shares, tensors, half_share_send),
-            (half_totals, 2, half_total_send),
-            (quarter_shares, tensors, quarter_share_send),
-            (quarter_totals, 4, quarter_total_send),
-            (gram_shares, tensors, gram_share_send),
-            (gram_parts, 4, gram_part_send),
-            (gram_totals, groups, gram_total_send),
+            (half_sums, pair_size, half_sum_send),
+            (quarter_sums, cluster_size, quarter_sum_send),
         ):
             wait_bytes(slots.at[chunk, pl.ds(0, size - 1)], sent.at[chunk])
         pltpu.make_async_copy(gathered_v.at[chunk], gathered.at[chunk], out_sem.at[chunk]).wait()
+    for slots, size, sent in (
+        (gram_parts, cluster_size, gram_part_send),
+        (gram_totals, groups, gram_total_send),
+    ):
+        wait_bytes(slots.at[0, pl.ds(0, size - 1)], sent.at[0])
 
 
 def level_by_level(vectors):
@@ -425,6 +438,11 @@
         up = lower_weight(totals[0], totals[2])[:, None, None]
         vectors = low * lower + up * upper
     return vectors.reshape(1, -1)
+
+
+def hand_on(*refs):
+    for source, target in zip(refs[: len(refs) // 2], refs[len(refs) // 2 :]):
+        target[...] = source[...]
 
 
 def per_device(*grads):
@@ -462,15 +480,14 @@
             pltpu.VMEM((chunks, 8, LANES), f32),
         ]
         + [
-            pltpu.VMEM((chunks, size, 8, LANES), f32)
-            for size in (tensors, 2, tensors, 4, tensors, 4, groups)
+            pltpu.VMEM((chunks, size, 1, LANES), f32) for size in (2 * tensors, 4 * tensors)
         ]
+        + [pltpu.VMEM((1, size, 8, LANES), f32) for size in (4 * tensors, groups)]
         + [
             dma((len(grads),)),
-            dma((chunks, 2)),
-            dma((chunks, 2)),
         ]
-        + [dma((chunks,))] * 19,
+        + [dma((chunks, 2))] * 4
+        + [dma((chunks,))] * 11,
         compiler_params=pltpu.CompilerParams(
             collective_id=0, has_side_effects=True, vmem_limit_bytes=60 * 1024 * 1024
         ),
@@ -487,14 +504,20 @@
                 start += width
         return outputs
 
+    chosen = lax.cond(
+        flag[0] > 0.0,
+        again,
+        lambda combined, gathered: list(combined),
+        list(combined),
+        gathered,
+    )
     return tuple(
-        lax.cond(
-            flag[0] > 0.0,
-            again,
-            lambda combined, gathered: list(combined),
-            list(combined),
-            gathered,
-        )
+        pl.pallas_call(
+            hand_on,
+            out_shape=[jax.ShapeDtypeStruct(member.shape, f32) for member in chosen],
+            in_specs=[pl.BlockSpec(memory_space=pltpu.VMEM)] * len(chosen),
+            out_specs=[pl.BlockSpec(memory_space=pltpu.VMEM)] * len(chosen),
+        )(*chosen)
     )
 
 

time: 128 us -> 118 us (0.922)
  Pallas kernels: 125 us -> 116 us
  local copies, waits for them, and re-layouts: 2.38 us -> 0 us
    pallas_call x1, Pallas kernels: 125 us -> 115 us  [per_device(): pl.pallas_call(functools.partial(kernel, replicas, tensors, members, tile...]
    unnamed x4 -> x0, local copies, waits for them, and re-layouts: 2.38 us -> none
where the time goes in v3:
time: 118 us; the launch traced here: 117 us
  Pallas kernels  116 us (98%)
  between operations  1.34 us (1%)
    pallas_call x1, Pallas kernels, per_device(): pl.pallas_call(functools.partial(kernel, replicas, tensors, members, tile...  115 us

profile of v3, /device:TPU:1, one launch (start us, length us, event | category | flops | bytes accessed | tf_op | source)
XLA Modules:
  0.0 117.4 jit_solution(6247255281526949066)
XLA Ops:
  0.6 115.5 %shard_map.75 = (f32[1,2304]{1,0:T(1,128)S(1)}, f32[1,768]{1,0:T(1,128)S(1)}, f32[1,3072]{1,0:T(1,128)S(1)}, f32[1,3072]{1,0:T(1,128)S(1)}, f32[3,384,128]{2,1,0:T(8,128)S(1)}, /*index=5*/f32[1]{0:T(128)}) custom-call(f32[1,64,2304]{2,1,0:T(8,128)} %refs_0_.1, f32[1,64,768]{2,1,0:T(8,128)} %refs_1_.1, f32[1,64,3072]{2,1,0:T(8,128)} %refs_2_.1, ...), custom_call_target="tpu_custom_call" | custom-call | tf_op jit(solution)/shard_map/pallas_call | solution.py:462
  116.8 0.6 shard_map.76
  (1 shorter events, 0.0 us)

commit v4 on v3

--- a/solution.py
+++ b/solution.py
@@ -13,8 +13,8 @@
 MESH = pl.DeviceIdType.MESH
 ORDER = (
     "s0A", "s1A", "b0B", "s0B", "b0C", "r0A", "s1B", "c0A", "q1A", "r0B", "s0C", "s1C", "r1A",
-    "c0B", "q1B", "r0C", "c1A", "r1B", "c0C", "w1A", "q1C", "c1B", "r1C", "w1B", "c1C", "w1C",
-    "r2A", "r2B", "r2C", "g2C", "u2C", "f2C",
+    "c0B", "q1B", "r0C", "c1A", "r1B", "c0C", "q1C", "w1A", "r1C", "c1B", "w1B", "c1C", "w1C",
+    "r2A", "r2B", "r2C", "g2C", "e2C", "u2C", "f2C",
 )
 
 
@@ -103,8 +103,6 @@
 
         lax.fori_loop(1, size, one, 0)
 
-    greet(cluster_size, cluster_me, cluster_device)
-    greet(groups, group, group_device)
 
     input_copies = []
     number = 0
@@ -123,6 +121,9 @@
     for copy in input_copies:
         copy.start()
 
+    greet(cluster_size, cluster_me, cluster_device)
+    greet(groups, group, group_device)
+
     rows_of_tile = lax.broadcasted_iota(jnp.int32, (tiles, LANES), 0)
     lane = lax.broadcasted_iota(jnp.int32, (1, LANES), 1)
 
@@ -168,19 +169,27 @@
             device_id_type=MESH,
         )
 
-    def broadcast(chunk, slots, size, me, device, send_sem, recv_sem):
-        def one(step, carry):
+    def broadcast(chunk, slots, size, near, me, device, send_sem, recv_sem):
+        def send(index):
             pltpu.make_async_remote_copy(
                 src_ref=slots.at[chunk, me],
                 dst_ref=slots.at[chunk, me],
                 send_sem=send_sem.at[chunk],
                 recv_sem=recv_sem.at[chunk],
-                device_id=device((me + step) % size),
+                device_id=device(index),
                 device_id_type=MESH,
             ).start()
+
+        def along_z(step, carry):
+            send(((me // near + 1) * near + step) % size)
             return carry
 
-        lax.fori_loop(1, size, one, 0)
+        def at_one_z(step, carry):
+            send(me // near * near + (me + step) % near)
+            return carry
+
+        lax.fori_loop(0, size - near, along_z, 0)
+        lax.fori_loop(1, near, at_one_z, 0)
 
     def wait_bytes(ref, semaphore):
         pltpu.make_async_copy(ref, ref, semaphore).wait()
@@ -253,7 +262,7 @@
         half_sums[chunk, pair_me] = statistics(
             chunk, lambda step: [half_pair(chunk, part, step) for part in range(2)], bit == 0
         )
-        broadcast(chunk, half_sums, pair_size, pair_me, pair_device, half_sum_send, half_sum_recv)
+        broadcast(chunk, half_sums, pair_size, tensors, pair_me, pair_device, half_sum_send, half_sum_recv)
 
     def half_combine(chunk):
         total = collect(chunk, half_sums, pair_size, half_sum_recv)
@@ -283,7 +292,7 @@
             chunk, lambda step: [quarter_pair(chunk, step)], high == 0
         )
         broadcast(
-            chunk, quarter_sums, cluster_size, cluster_me, cluster_device, quarter_sum_send, quarter_sum_recv
+            chunk, quarter_sums, cluster_size, tensors, cluster_me, cluster_device, quarter_sum_send, quarter_sum_recv
         )
 
     def quarter_combine(chunk):
@@ -355,12 +364,26 @@
             total = total + grams[chunk]
         gram_parts[0, cluster_me] = total
         broadcast(
-            0, gram_parts, cluster_size, cluster_me, cluster_device, gram_part_send, gram_part_recv
-        )
+            0, gram_parts, cluster_size, tensors, cluster_me, cluster_device, gram_part_send, gram_part_recv
+        )
+
+    def settle(_):
+        for chunk in range(chunks):
+            for part in range(2):
+                half_copy(part, chunk).wait_send()
+            for part in range(2):
+                quarter_copy(part, chunk).wait_send()
+            wait_bytes(gathered_v.at[chunk, pl.ds(0, (groups - 1) * tiles)], row_send.at[chunk])
+            for slots, size, sent in (
+                (half_sums, pair_size, half_sum_send),
+                (quarter_sums, cluster_size, quarter_sum_send),
+            ):
+                wait_bytes(slots.at[chunk, pl.ds(0, size - 1)], sent.at[chunk])
+            pltpu.make_async_copy(gathered_v.at[chunk], gathered.at[chunk], out_sem.at[chunk]).wait()
 
     def gram_total(_):
         gram_totals[0, group] = collect(0, gram_parts, cluster_size, gram_part_recv)
-        broadcast(0, gram_totals, groups, group, group_device, gram_total_send, gram_total_recv)
+        broadcast(0, gram_totals, groups, 1, group, group_device, gram_total_send, gram_total_recv)
 
     def finish(_):
         total = collect(0, gram_totals, groups, gram_total_recv)
@@ -396,24 +419,13 @@
         "w1": send_rows,
         "r2": gram_of,
         "g2": gram_part,
+        "e2": settle,
         "u2": gram_total,
         "f2": finish,
     }
     for step in ORDER:
         steps[step[:2]]("ABC".index(step[2]))
 
-    for chunk in range(chunks):
-        for part in range(2):
-            half_copy(part, chunk).wait_send()
-        for part in range(2):
-            quarter_copy(part, chunk).wait_send()
-        wait_bytes(gathered_v.at[chunk, pl.ds(0, (groups - 1) * tiles)], row_send.at[chunk])
-        for slots, size, sent in (
-            (half_sums, pair_size, half_sum_send),
-            (quarter_sums, cluster_size, quarter_sum_send),
-        ):
-            wait_bytes(slots.at[chunk, pl.ds(0, size - 1)], sent.at[chunk])
-        pltpu.make_async_copy(gathered_v.at[chunk], gathered.at[chunk], out_sem.at[chunk]).wait()
     for slots, size, sent in (
         (gram_parts, cluster_size, gram_part_send),
         (gram_totals, groups, gram_total_send),

time: 118 us -> 116 us (0.983)
    pallas_call x1, Pallas kernels: 115 us -> 114 us  [per_device(): pl.pallas_call(functools.partial(kernel, replicas, tensors, members, tile...]
where the time goes in v4:
time: 116 us
  Pallas kernels  115 us (99%)
  between operations  1.34 us (1%)
    pallas_call x1, Pallas kernels, per_device(): pl.pallas_call(functools.partial(kernel, replicas, tensors, members, tile...  114 us

profile of v4, /device:TPU:1, one launch (start us, length us, event | category | flops | bytes accessed | tf_op | source)
XLA Modules:
  0.0 116.0 jit_solution(11096272953064867550)
XLA Ops:
  0.6 114.1 %shard_map.75 = (f32[1,2304]{1,0:T(1,128)S(1)}, f32[1,768]{1,0:T(1,128)S(1)}, f32[1,3072]{1,0:T(1,128)S(1)}, f32[1,3072]{1,0:T(1,128)S(1)}, f32[3,384,128]{2,1,0:T(8,128)S(1)}, /*index=5*/f32[1]{0:T(128)}) custom-call(f32[1,64,2304]{2,1,0:T(8,128)} %refs_0_.1, f32[1,64,768]{2,1,0:T(8,128)} %refs_1_.1, f32[1,64,3072]{2,1,0:T(8,128)} %refs_2_.1, ...), custom_call_target="tpu_custom_call" | custom-call | tf_op jit(solution)/shard_map/pallas_call | solution.py:474
  115.4 0.6 shard_map.76
  (1 shorter events, 0.0 us)
